TPU v7x, 32 devices: a whole 2x2x4 slice. The times are simulated.
32 devices in a mesh: fit: 8 (over z, core), orb: 4 (over y, x).
Axes of the slice: x: 2, y: 2, z: 4, core: 2. Of those that a mesh axis runs over, the one named last changes fastest.
Arguments:
- half_ints: bfloat16 [4, 64, 768, 256], P('orb', None, 'fit'), may hold values from -6 to 6
- osv_coef: bfloat16 [4, 64, 256, 64], P('orb', 'fit'), may hold values from -0.09375 to 0.09375
- fit_blocks: int32 [4, 64, 6], P('orb', 'fit'), may hold values from 0 to 468, as said below
- partner_list: int32 [8, 4, 24], P('fit'), may hold values from 0 to 31, as said below
Outputs:
- pair_ints: bfloat16 [4, 64, 24, 4096], P('orb', 'fit')
Inputs may be any that keep to these rules, and one draw needn't show every extreme that they name: `fit_blocks`: the 6 block numbers of one orbital are distinct. `partner_list`: entry h * 8 + k names orbital k of the same column in group h. The 24 entries of one list are distinct. Of one list, at most 8 entries name orbitals of any one group, and in every list some group is named exactly 8 times.
All inputs are finite; a program needn't handle non-finite values.
Results may differ from a plain program's by a relative error of at most 0.0055.
Values may be sent and summed in bfloat16 or wider, within the bound.
A program may use at most 64 MiB of HBM per device.

v0:
```python
import jax
import jax.numpy as jnp
from jax import lax
from jax.sharding import PartitionSpec as P

BLK = 128
FBLK = 6


def per_device(half_ints, osv_coef, fit_blocks, partner_list):
    local_rows = half_ints[0]
    own_ints = lax.all_to_all(local_rows, "fit", split_axis=0, concat_axis=1, tiled=True)
    osv_local = osv_coef[0]
    projected = jnp.einsum(
        "kfa,kao->kof", own_ints, osv_local, preferred_element_type=jnp.float32
    ).astype(jnp.bfloat16)
    own_blocks = fit_blocks[0]
    column_lists = partner_list[0]
    nosv_count = projected.shape[1]
    npart_count = column_lists.shape[1]
    my_group = lax.axis_index("orb")
    wanted = lax.dynamic_index_in_dim(column_lists, my_group, 0, keepdims=False)
    piece_rows = lax.all_gather(projected, "orb", axis=0, tiled=True)
    piece_blocks = lax.all_gather(own_blocks, "orb", axis=0, tiled=True)
    piece_len = piece_rows.shape[0]
    matches = wanted[:, None] == jnp.arange(piece_len, dtype=jnp.int32)[None, :]
    buffer = jnp.einsum(
        "nr,rxf->nxf", matches.astype(jnp.bfloat16), piece_rows, preferred_element_type=jnp.float32
    ).astype(jnp.bfloat16)
    blocks = jnp.sum(jnp.where(matches[:, :, None], piece_blocks[None, :, :], 0), axis=1).astype(
        jnp.int32
    )
    partner_pieces = buffer.reshape(npart_count, nosv_count, FBLK, BLK)

    def pair_block(operand):
        own_rows, own_ids = operand
        matching = (own_ids[None, :, None] == blocks[:, None, :]).astype(jnp.bfloat16)
        aligned = jnp.einsum(
            "nbc,nxcp->nxbp", matching, partner_pieces, preferred_element_type=jnp.float32
        ).astype(jnp.bfloat16)
        pair_vals = jnp.einsum(
            "abp,nxbp->nax",
            own_rows.reshape(nosv_count, FBLK, BLK),
            aligned,
            preferred_element_type=jnp.float32,
        )
        return pair_vals.astype(jnp.bfloat16).reshape(npart_count, nosv_count * nosv_count)

    result = lax.map(pair_block, (projected, own_blocks))
    return result[None]


def solution(mesh):
    return jax.shard_map(
        per_device,
        mesh=mesh,
        in_specs=(
            P("orb", None, "fit", None),
            P("orb", "fit", None, None),
            P("orb", "fit", None),
            P("fit", None, None),
        ),
        out_specs=P("orb", "fit", None, None),
        check_vma=False,
    )
```

profile of v0, /device:TPU:0, one launch (start us, length us, event | category | flops | bytes accessed | tf_op | source)
XLA Modules:
  0.0 254.9 jit_solution(2960780076971399511)
XLA Ops:
  6.5 78.0 %all_to_all.18 = bf16[64,96,256]{2,1,0:T(8,128)(2,1)S(1)} all-to-all(bf16[64,96,256]{2,1,0:T(8,128)(2,1)} %bitcast.55), channel_id=1, replica_groups=mesh['fit'=8,'orb'=4] {'fit'}, dimensions={0} | all-to-all | bytes 6291456 | tf_op jit(solution)/shard_map/all_to_all | solution.py:12
  84.8 1.9 convolution_convert_fusion
  87.0 8.2 %all-gather = s32[1,32,6]{2,0,1:T(1,128)S(1)} all-gather(s32[1,8,6]{2,0,1:T(1,128)S(1)} %copy.31), channel_id=2, replica_groups=mesh['fit'=8,'orb'=4] {'orb'}, dimensions={1}, use_global_device_ids=true | all-gather | bytes 960 | tf_op jit(solution)/shard_map/all_gather | solution.py:24
  96.2 33.6 %all-gather.3.cloned.1.call-done = bf16[32,64,768]{2,1,0:T(8,128)(2,1)} async-done(((bf16[8,64,768]{2,1,0:T(8,128)(2,1)}), bf16[32,64,768]{2,1,0:T(8,128)(2,1)}) %all-gather.3.cloned.1.call-update) | async-done | bytes 3145744 | tf_op jit(solution)/shard_map/all_gather | solution.py:23
  129.8 4.5 %fusion.20 = bf16[24,64,768]{2,0,1:T(8,128)(2,1)S(1)} fusion(bf16[32,64,768]{2,1,0:T(8,128)(2,1)} %all-gather.3.cloned.1.call-done, s32[24]{0:T(128)S(1)} %dynamic-slice_bitcast_fusion), kind=kOutput, calls=%fused_computation.18 | convolution fusion | flops 76677888 | bytes 5505120 | tf_op jit(solution)/shard_map/nr,rxf->nxf/dot_general | solution.py:27
  134.3 1.9 copy.35
  136.3 4.8 %reshape.40 = bf16[24,64,6,128]{3,2,1,0:T(8,128)(2,1)S(1)} reshape(bf16[24,64,768]{2,1,0:T(8,128)(2,1)} %copy.35) | data formatting | bytes 4718592 | tf_op jit(solution)/shard_map/reshape | solution.py:33
  141.1 106.9 %while.10 = (s32[]{:T(128)}, bf16[8,24,4096]{2,1,0:T(8,128)(2,1)}, s32[8,6]{1,0:T(8,128)S(1)}, s32[24,6]{1,0:T(8,128)S(1)}, bf16[24,64,6,128]{3,2,1,0:T(8,128)(2,1)S(1)}, /*index=5*/bf16[8,64,768]{2,1,0:T(8,128)(2,1)}, s32[]{:T(128)}) while((s32[]{:T(128)}, bf16[8,24,4096]{2,1,0:T(8,128)(2,1)}, s32[8,6]{1,0:T(8,128)S(1)}, ...), condition=%wide.region_2.3_spmd, body=%wide.region_1.2_spmd.sunk | while | flops 166429536 | bytes 8946909 | solution.py:49
  141.1 2.7 %convert_bitcast_fusion.2 = bf16[24,64,6,128]{3,2,1,0:T(8,128)(2,1)} fusion(bf16[24,64,6,128]{3,2,1,0:T(8,128)(2,1)S(1)} %get-tuple-element.117, s32[24,6]{1,0:T(8,128)S(1)} %get-tuple-element.116, s32[6]{0:T(128)S(1)} %fusion.37), kind=kOutput, calls=%fused_computation.clone.1 | convolution fusion | flops 15336288 | bytes 4719192 | tf_op jit(solution)/shard_map/while/body/eval_jaxpr/nbc,nxcp->nxbp/dot_general | solution.py:38
  145.5 3.4 %fusion.38 = bf16[24,64,64]{1,2,0:T(8,128)(2,1)} fusion(bf16[24,64,6,128]{3,2,1,0:T(8,128)(2,1)} %convert_bitcast_fusion.2, bf16[64,6,128]{2,1,0:T(8,128)(2,1)} %reshape.47), kind=kOutput, calls=%fused_computation.5.clone.1 | convolution fusion | flops 151093248 | bytes 2654208 | tf_op jit(solution)/shard_map/while/body/eval_jaxpr/abp,nxbp->nax/dot_general | solution.py:41
  150.8 2.0 broadcast_in_dim.45
  154.5 2.7 %convert_bitcast_fusion.2 = bf16[24,64,6,128]{3,2,1,0:T(8,128)(2,1)} fusion(bf16[24,64,6,128]{3,2,1,0:T(8,128)(2,1)S(1)} %get-tuple-element.117, s32[24,6]{1,0:T(8,128)S(1)} %get-tuple-element.116, s32[6]{0:T(128)S(1)} %fusion.37), kind=kOutput, calls=%fused_computation.clone.1 | convolution fusion | flops 15336288 | bytes 4719192 | tf_op jit(solution)/shard_map/while/body/eval_jaxpr/nbc,nxcp->nxbp/dot_general | solution.py:38
  158.8 3.4 %fusion.38 = bf16[24,64,64]{1,2,0:T(8,128)(2,1)} fusion(bf16[24,64,6,128]{3,2,1,0:T(8,128)(2,1)} %convert_bitcast_fusion.2, bf16[64,6,128]{2,1,0:T(8,128)(2,1)} %reshape.47), kind=kOutput, calls=%fused_computation.5.clone.1 | convolution fusion | flops 151093248 | bytes 2654208 | tf_op jit(solution)/shard_map/while/body/eval_jaxpr/abp,nxbp->nax/dot_general | solution.py:41
  164.2 2.0 broadcast_in_dim.45
  167.8 2.7 %convert_bitcast_fusion.2 = bf16[24,64,6,128]{3,2,1,0:T(8,128)(2,1)} fusion(bf16[24,64,6,128]{3,2,1,0:T(8,128)(2,1)S(1)} %get-tuple-element.117, s32[24,6]{1,0:T(8,128)S(1)} %get-tuple-element.116, s32[6]{0:T(128)S(1)} %fusion.37), kind=kOutput, calls=%fused_computation.clone.1 | convolution fusion | flops 15336288 | bytes 4719192 | tf_op jit(solution)/shard_map/while/body/eval_jaxpr/nbc,nxcp->nxbp/dot_general | solution.py:38
  172.2 3.4 %fusion.38 = bf16[24,64,64]{1,2,0:T(8,128)(2,1)} fusion(bf16[24,64,6,128]{3,2,1,0:T(8,128)(2,1)} %convert_bitcast_fusion.2, bf16[64,6,128]{2,1,0:T(8,128)(2,1)} %reshape.47), kind=kOutput, calls=%fused_computation.5.clone.1 | convolution fusion | flops 151093248 | bytes 2654208 | tf_op jit(solution)/shard_map/while/body/eval_jaxpr/abp,nxbp->nax/dot_general | solution.py:41
  177.5 2.0 broadcast_in_dim.45
  181.2 2.7 %convert_bitcast_fusion.2 = bf16[24,64,6,128]{3,2,1,0:T(8,128)(2,1)} fusion(bf16[24,64,6,128]{3,2,1,0:T(8,128)(2,1)S(1)} %get-tuple-element.117, s32[24,6]{1,0:T(8,128)S(1)} %get-tuple-element.116, s32[6]{0:T(128)S(1)} %fusion.37), kind=kOutput, calls=%fused_computation.clone.1 | convolution fusion | flops 15336288 | bytes 4719192 | tf_op jit(solution)/shard_map/while/body/eval_jaxpr/nbc,nxcp->nxbp/dot_general | solution.py:38
  185.6 3.4 %fusion.38 = bf16[24,64,64]{1,2,0:T(8,128)(2,1)} fusion(bf16[24,64,6,128]{3,2,1,0:T(8,128)(2,1)} %convert_bitcast_fusion.2, bf16[64,6,128]{2,1,0:T(8,128)(2,1)} %reshape.47), kind=kOutput, calls=%fused_computation.5.clone.1 | convolution fusion | flops 151093248 | bytes 2654208 | tf_op jit(solution)/shard_map/while/body/eval_jaxpr/abp,nxbp->nax/dot_general | solution.py:41
  190.9 2.0 broadcast_in_dim.45
  194.6 2.7 %convert_bitcast_fusion.2 = bf16[24,64,6,128]{3,2,1,0:T(8,128)(2,1)} fusion(bf16[24,64,6,128]{3,2,1,0:T(8,128)(2,1)S(1)} %get-tuple-element.117, s32[24,6]{1,0:T(8,128)S(1)} %get-tuple-element.116, s32[6]{0:T(128)S(1)} %fusion.37), kind=kOutput, calls=%fused_computation.clone.1 | convolution fusion | flops 15336288 | bytes 4719192 | tf_op jit(solution)/shard_map/while/body/eval_jaxpr/nbc,nxcp->nxbp/dot_general | solution.py:38
  198.9 3.4 %fusion.38 = bf16[24,64,64]{1,2,0:T(8,128)(2,1)} fusion(bf16[24,64,6,128]{3,2,1,0:T(8,128)(2,1)} %convert_bitcast_fusion.2, bf16[64,6,128]{2,1,0:T(8,128)(2,1)} %reshape.47), kind=kOutput, calls=%fused_computation.5.clone.1 | convolution fusion | flops 151093248 | bytes 2654208 | tf_op jit(solution)/shard_map/while/body/eval_jaxpr/abp,nxbp->nax/dot_general | solution.py:41
  204.3 2.0 broadcast_in_dim.45
  207.9 2.7 %convert_bitcast_fusion.2 = bf16[24,64,6,128]{3,2,1,0:T(8,128)(2,1)} fusion(bf16[24,64,6,128]{3,2,1,0:T(8,128)(2,1)S(1)} %get-tuple-element.117, s32[24,6]{1,0:T(8,128)S(1)} %get-tuple-element.116, s32[6]{0:T(128)S(1)} %fusion.37), kind=kOutput, calls=%fused_computation.clone.1 | convolution fusion | flops 15336288 | bytes 4719192 | tf_op jit(solution)/shard_map/while/body/eval_jaxpr/nbc,nxcp->nxbp/dot_general | solution.py:38
  212.3 3.4 %fusion.38 = bf16[24,64,64]{1,2,0:T(8,128)(2,1)} fusion(bf16[24,64,6,128]{3,2,1,0:T(8,128)(2,1)} %convert_bitcast_fusion.2, bf16[64,6,128]{2,1,0:T(8,128)(2,1)} %reshape.47), kind=kOutput, calls=%fused_computation.5.clone.1 | convolution fusion | flops 151093248 | bytes 2654208 | tf_op jit(solution)/shard_map/while/body/eval_jaxpr/abp,nxbp->nax/dot_general | solution.py:41
  217.6 2.0 broadcast_in_dim.45
  221.3 2.7 %convert_bitcast_fusion.2 = bf16[24,64,6,128]{3,2,1,0:T(8,128)(2,1)} fusion(bf16[24,64,6,128]{3,2,1,0:T(8,128)(2,1)S(1)} %get-tuple-element.117, s32[24,6]{1,0:T(8,128)S(1)} %get-tuple-element.116, s32[6]{0:T(128)S(1)} %fusion.37), kind=kOutput, calls=%fused_computation.clone.1 | convolution fusion | flops 15336288 | bytes 4719192 | tf_op jit(solution)/shard_map/while/body/eval_jaxpr/nbc,nxcp->nxbp/dot_general | solution.py:38
  225.7 3.4 %fusion.38 = bf16[24,64,64]{1,2,0:T(8,128)(2,1)} fusion(bf16[24,64,6,128]{3,2,1,0:T(8,128)(2,1)} %convert_bitcast_fusion.2, bf16[64,6,128]{2,1,0:T(8,128)(2,1)} %reshape.47), kind=kOutput, calls=%fused_computation.5.clone.1 | convolution fusion | flops 151093248 | bytes 2654208 | tf_op jit(solution)/shard_map/while/body/eval_jaxpr/abp,nxbp->nax/dot_general | solution.py:41
  231.0 2.0 broadcast_in_dim.45
  234.7 2.7 %convert_bitcast_fusion.2 = bf16[24,64,6,128]{3,2,1,0:T(8,128)(2,1)} fusion(bf16[24,64,6,128]{3,2,1,0:T(8,128)(2,1)S(1)} %get-tuple-element.117, s32[24,6]{1,0:T(8,128)S(1)} %get-tuple-element.116, s32[6]{0:T(128)S(1)} %fusion.37), kind=kOutput, calls=%fused_computation.clone.1 | convolution fusion | flops 15336288 | bytes 4719192 | tf_op jit(solution)/shard_map/while/body/eval_jaxpr/nbc,nxcp->nxbp/dot_general | solution.py:38
  239.0 3.4 %fusion.38 = bf16[24,64,64]{1,2,0:T(8,128)(2,1)} fusion(bf16[24,64,6,128]{3,2,1,0:T(8,128)(2,1)} %convert_bitcast_fusion.2, bf16[64,6,128]{2,1,0:T(8,128)(2,1)} %reshape.47), kind=kOutput, calls=%fused_computation.5.clone.1 | convolution fusion | flops 151093248 | bytes 2654208 | tf_op jit(solution)/shard_map/while/body/eval_jaxpr/abp,nxbp->nax/dot_general | solution.py:41
  244.4 2.0 broadcast_in_dim.45
  (55 shorter events, 43.4 us)
Async XLA Ops:
  6.5 78.3 %copy-start = (bf16[1,8,256,64]{2,3,1,0:T(8,128)(2,1)S(1)}, bf16[1,8,256,64]{2,3,1,0:T(8,128)(2,1)}, u32[]{:S(2)}) copy-start(bf16[1,8,256,64]{2,3,1,0:T(8,128)(2,1)} %param.7) | copy-start | bytes 786436
  6.5 123.3 %all-gather.3.cloned.1.call-start = ((), (), s32[]{:S(2)}) async-start(), calls=%async_computation.1 | async-start | bytes 3932160 | tf_op jit(solution)/shard_map/all_gather | solution.py:23
  84.8 2.0 copy-start.1
Sparse Core Ops, SparseCore 0:
  86.9 42.8 all-gather.2
where the time goes:
time: 256 us; the launch traced here: 255 us
  blocking collectives  86.1 us (34%)
  local copies, waits for them, and re-layouts  66.1 us (26%)
  matrix products  55.2 us (22%)
  waiting for transfers between devices  33.6 us (13%)
  between operations  13.5 us (5%)
    all_to_all x1, blocking collectives, per_device(): lax.all_to_all(local_rows, 'fit', split_axis=0, concat_axis=1, tiled=True)  78 us
    all_gather x1, waiting for transfers between devices, per_device(): piece_rows = lax.all_gather(projected, 'orb', axis=0, tiled=True)  33.6 us
    dot_general x8, matrix products, pair_block(): jnp.einsum('abp,nxbp->nax', own_rows.reshape(nosv_count, FBLK, BLK), alig...  27.3 us
    dot_general x8, matrix products, pair_block(): jnp.einsum('nbc,nxcp->nxbp', matching, partner_pieces, preferred_element_...  21.5 us
    broadcast_in_dim x8, local copies, waits for them, and re-layouts, per_device(): result = lax.map(pair_block, (projected, own_blocks))  16.3 us
    convert_element_type x8, local copies, waits for them, and re-layouts, pair_block(): pair_vals.astype(jnp.bfloat16).reshape(npart_count, nosv_count * nosv_count)  15.4 us
    dynamic_update_slice x8, local copies, waits for them, and re-layouts, per_device(): result = lax.map(pair_block, (projected, own_blocks))  12.9 us
    all_gather x1, blocking collectives, per_device(): piece_blocks = lax.all_gather(own_blocks, 'orb', axis=0, tiled=True)  8.15 us
  transfers between devices with their start and end apart: 1, of which 1 were waited for; matrix products, arithmetic and copies ran while one was open for 0% of the time, Pallas kernels for 0%

commit v1 on v0

v1 whole, which is shorter than its diff:
```python
import functools

import jax
import jax.numpy as jnp
from jax import lax
from jax.experimental import pallas as pl
from jax.experimental.pallas import tpu as pltpu
from jax.sharding import PartitionSpec as P

BLK = 128


def pair_kernel(sizes, wanted_ref, index_ref, own_ref, all_ref, out_ref, turned, staged):
    pairs, nosv, fblk, npart = sizes
    orbs = 2 * pairs
    half = nosv // 2
    lanes = 2 * nosv
    row = lax.broadcasted_iota(jnp.int32, (lanes, lanes), 0)
    col = lax.broadcasted_iota(jnp.int32, (lanes, lanes), 1)
    inner = row % nosv
    source = (row // nosv) * nosv + (inner % half) * 2 + inner // half
    order = jnp.where(col == source, 1.0, 0.0).astype(jnp.bfloat16)
    for q in range(pairs):
        flipped = lax.dot_general(
            order, own_ref[q], (((1,), (1,)), ((), ())), preferred_element_type=jnp.float32
        ).astype(jnp.bfloat16)
        for s in range(2):
            for b in range(fblk):
                turned[2 * q + s, b] = flipped[s * nosv:(s + 1) * nosv, b * BLK:(b + 1) * BLK]
            turned[2 * q + s, fblk] = jnp.zeros((nosv, BLK), jnp.bfloat16)

    lane = lax.broadcasted_iota(jnp.int32, (half, lanes), 1)
    low = lane < nosv

    @pl.loop(0, npart)
    def _(n):
        w = wanted_ref[n]
        slab = w // 2
        odd = (w % 2) == 1
        rhs = all_ref[slab]
        lhs = jnp.concatenate(
            [
                jnp.concatenate(
                    [turned[r, index_ref[(w * orbs + r) * fblk + e]] for e in range(fblk)], axis=1
                )
                for r in range(orbs)
            ],
            axis=0,
        )
        vals = jnp.dot(lhs, rhs, preferred_element_type=jnp.float32)
        keep_low = jnp.logical_xor(low, odd)
        for r in range(orbs):
            even_rows = vals[r * nosv:r * nosv + half]
            odd_rows = vals[r * nosv + half:(r + 1) * nosv]
            moved = pltpu.roll(jnp.where(odd, even_rows, odd_rows), nosv, 1)
            kept = jnp.where(odd, odd_rows, even_rows)
            staged[r, pl.ds(n, half, stride=npart), :] = jnp.where(keep_low, kept, moved)

    for r in range(orbs):
        for j in range(half):
            out_ref[r, :, j * lanes:(j + 1) * lanes] = staged[
                r, j * npart:(j + 1) * npart, :
            ].astype(jnp.bfloat16)


def pair_integrals(own, gathered, own_blocks, all_blocks, wanted):
    pairs, depth, lanes = own.shape
    nosv = lanes // 2
    orbs, fblk = own_blocks.shape
    npart = wanted.shape[0]
    count = all_blocks.shape[0]
    hits = all_blocks[:, None, :, None] == own_blocks[None, :, None, :]
    numbers = jnp.arange(fblk, dtype=jnp.int32)
    index = fblk + jnp.sum(jnp.where(hits, numbers - fblk, 0), axis=3, dtype=jnp.int32)
    return pl.pallas_call(
        functools.partial(pair_kernel, (pairs, nosv, fblk, npart)),
        out_shape=jax.ShapeDtypeStruct((orbs, npart, nosv * nosv), jnp.bfloat16),
        in_specs=[
            pl.BlockSpec(memory_space=pltpu.SMEM),
            pl.BlockSpec(memory_space=pltpu.SMEM),
            pl.BlockSpec(memory_space=pltpu.VMEM),
            pl.BlockSpec(memory_space=pltpu.VMEM),
        ],
        out_specs=pl.BlockSpec(memory_space=pltpu.VMEM),
        scratch_shapes=[
            pltpu.VMEM((orbs, fblk + 1, nosv, BLK), jnp.bfloat16),
            pltpu.VMEM((orbs, (nosv // 2) * npart, lanes), jnp.float32),
        ],
        compiler_params=pltpu.CompilerParams(vmem_limit_bytes=48 << 20),
        cost_estimate=pl.CostEstimate(
            flops=2 * npart * orbs * nosv * lanes * depth,
            bytes_accessed=2 * (own.size + gathered.size + orbs * npart * nosv * nosv),
            transcendentals=0,
        ),
    )(wanted, index.reshape(count * orbs * fblk), own, gathered)


def exchange(rows, osv):
    own_ints = lax.all_to_all(rows, "fit", split_axis=0, concat_axis=1, tiled=True)
    orbs, depth = own_ints.shape[:2]
    nosv = osv.shape[-1]
    projected = jnp.einsum(
        "kfa,kao->kfo", own_ints, osv, preferred_element_type=jnp.float32
    ).astype(jnp.bfloat16)
    own = (
        projected.reshape(orbs // 2, 2, depth, nosv)
        .transpose(0, 2, 1, 3)
        .reshape(orbs // 2, depth, 2 * nosv)
    )
    return own, lax.all_gather(own, "orb", axis=0, tiled=True)


def per_device(half_ints, osv_coef, fit_blocks, partner_list):
    own_blocks = fit_blocks[0]
    my_group = lax.axis_index("orb")
    wanted = lax.dynamic_index_in_dim(partner_list[0], my_group, 0, keepdims=False)
    all_blocks = lax.all_gather(own_blocks, "orb", axis=0, tiled=True)
    own, gathered = exchange(half_ints[0], osv_coef[0])
    return pair_integrals(own, gathered, own_blocks, all_blocks, wanted)[None]


def solution(mesh):
    return jax.shard_map(
        per_device,
        mesh=mesh,
        in_specs=(
            P("orb", None, "fit", None),
            P("orb", "fit", None, None),
            P("orb", "fit", None),
            P("fit", None, None),
        ),
        out_specs=P("orb", "fit", None, None),
        check_vma=False,
    )
```

time: 256 us -> 153 us (0.60)
  local copies, waits for them, and re-layouts: 66.1 us -> 5.58 us
  matrix products: 55.2 us -> 1.07 us
  Pallas kernels: 0 us -> 13 us
    dot_general x18 -> x1, matrix products: 55.2 us -> 1.07 us  [exchange(): jnp.einsum('kfa,kao->kfo', own_ints, osv, preferred_element_type=jnp.floa...]
    convert_element_type x9 -> x0, local copies, waits for them, and re-layouts: 17.3 us -> none  [the longest x8 15.4 us: pair_block(): pair_vals.astype(jnp.bfloat16).reshape(npart_count, nosv_count * nosv_count)]
    broadcast_in_dim x8 -> x0, local copies, waits for them, and re-layouts: 16.3 us -> none  [per_device(): result = lax.map(pair_block, (projected, own_blocks))]
    pallas_call x0 -> x1, Pallas kernels: none -> 13 us  [pair_integrals(): pl.pallas_call(functools.partial(pair_kernel, (pairs, nosv, fblk, npart))...]
    dynamic_update_slice x8 -> x0, local copies, waits for them, and re-layouts: 12.9 us -> none  [per_device(): result = lax.map(pair_block, (projected, own_blocks))]
    reshape x9 -> x1, local copies, waits for them, and re-layouts: 11.1 us -> 1.16 us  [exchange(): own = projected.reshape(orbs // 2, 2, depth, nosv).transpose(0, 2, 1, 3)....]
    dynamic_slice x8 -> x0, local copies, waits for them, and re-layouts: 7.19 us -> none  [per_device(): result = lax.map(pair_block, (projected, own_blocks))]
    unnamed x6 -> x9, local copies, waits for them, and re-layouts: 0.17 us -> 3.11 us
  transfers between devices with their start and end apart: 1 -> 1, of which waited for: 1 -> 1; matrix products, arithmetic and copies ran while one was open for 0% -> 1% of each run, Pallas kernels for 0% -> 0%
where the time goes in v1:
time: 153 us
  blocking collectives  86.1 us (56%)
  waiting for transfers between devices  33.6 us (22%)
  between operations  13.5 us (9%)
  Pallas kernels  13 us (8%)
  local copies, waits for them, and re-layouts  5.58 us (4%)
    all_to_all x1, blocking collectives, exchange(): lax.all_to_all(rows, 'fit', split_axis=0, concat_axis=1, tiled=True)  78 us
    all_gather x1, waiting for transfers between devices, exchange(): return (own, lax.all_gather(own, 'orb', axis=0, tiled=True))  33.6 us
    pallas_call x1, Pallas kernels, pair_integrals(): pl.pallas_call(functools.partial(pair_kernel, (pairs, nosv, fblk, npart))...  13 us
    all_gather x1, blocking collectives, per_device(): all_blocks = lax.all_gather(own_blocks, 'orb', axis=0, tiled=True)  8.15 us
    unnamed x9, local copies, waits for them, and re-layouts  3.11 us
  transfers between devices with their start and end apart: 1, of which 1 were waited for; matrix products, arithmetic and copies ran while one was open for 1% of the time, Pallas kernels for 0%

profile of v1, /device:TPU:0, one launch (start us, length us, event | category | flops | bytes accessed | tf_op | source)
XLA Modules:
  0.0 153.0 jit_solution(2098243387398015393)
XLA Ops:
  6.5 0.0 copy-start
  6.5 0.0 all-gather.3.cloned.1.call-start
  6.5 78.0 %all_to_all.18 = bf16[64,96,256]{2,1,0:T(8,128)(2,1)S(1)} all-to-all(bf16[64,96,256]{2,1,0:T(8,128)(2,1)} %bitcast.25), channel_id=1, replica_groups=mesh['fit'=8,'orb'=4] {'fit'}, dimensions={0} | all-to-all | bytes 6291456 | tf_op jit(solution)/shard_map/all_to_all | solution.py:99
  84.5 0.3 copy.24
  84.8 0.0 copy-done
  84.8 0.0 copy-start.3
  84.8 1.1 convolution_convert_fusion
  85.9 1.2 copy.26.own_ref
  87.0 0.0 all-gather.3.cloned.1.call-update
  87.1 0.0 copy-done.3
  87.1 0.1 copy.19
  87.2 8.2 %all-gather = s32[1,32,6]{2,0,1:T(1,128)S(1)} all-gather(s32[1,8,6]{2,0,1:T(1,128)S(1)} %copy.19), channel_id=2, replica_groups=mesh['fit'=8,'orb'=4] {'orb'}, dimensions={1}, use_global_device_ids=true | all-gather | bytes 960 | tf_op jit(solution)/shard_map/all_gather | solution.py:117
  95.3 0.1 copy.20
  95.4 0.1 select_reduce_fusion
  95.5 0.1 copy.23
  95.7 0.1 add.18.index_ref
  95.8 0.7 dynamic-slice_bitcast_fusion.wanted_ref
  96.5 33.6 %all-gather.3.cloned.1.call-done.all_ref = bf16[16,768,128]{2,1,0:T(8,128)(2,1)} async-done(((bf16[4,768,128]{2,1,0:T(8,128)(2,1)}), bf16[16,768,128]{2,1,0:T(8,128)(2,1)}) %all-gather.3.cloned.1.call-update) | async-done | bytes 3145744 | tf_op jit(solution)/shard_map/all_gather | solution.py:110
  130.1 0.0 copy-start.1
  130.1 1.1 copy-done.1
  131.3 0.0 copy-start.2
  131.3 1.9 %copy-done.2 = bf16[16,768,128]{2,1,0:T(8,128)(2,1)S(1)} copy-done((bf16[16,768,128]{2,1,0:T(8,128)(2,1)S(1)}, bf16[16,768,128]{2,1,0:T(8,128)(2,1)}, u32[]{:S(2)}) %copy-start.2) | copy-done | bytes 3145752
  133.1 13.0 %shard_map.46 = bf16[8,24,4096]{2,1,0:T(8,128)(2,1)} custom-call(s32[24]{0:T(128)S(1)} %dynamic-slice_bitcast_fusion.wanted_ref, s32[1536]{0:T(1024)S(1)} %add.18.index_ref, bf16[4,768,128]{2,1,0:T(8,128)(2,1)S(1)} %copy-done.1, bf16[16,768,128]{2,1,0:T(8,128)(2,1)S(1)} %copy-done.2), custom_call_target="tpu_custom_call" | custom-call | flops 2415919104 | bytes 5505024 | tf_op jit(solution)/shard_map/pallas_call | solution.py:75
  (3 shorter events, 0.0 us)
Async XLA Ops:
  6.5 78.3 %copy-start = (bf16[1,8,256,64]{2,3,1,0:T(8,128)(2,1)S(1)}, bf16[1,8,256,64]{2,3,1,0:T(8,128)(2,1)}, u32[]{:S(2)}) copy-start(bf16[1,8,256,64]{2,3,1,0:T(8,128)(2,1)} %param.5) | copy-start | bytes 786436
  6.5 123.6 %all-gather.3.cloned.1.call-start = ((), (), s32[]{:S(2)}) async-start(), calls=%async_computation.1 | async-start | bytes 3932160 | tf_op jit(solution)/shard_map/all_gather | solution.py:110
  84.8 2.3 %copy-start.3 = (s32[1,8,6]{1,0,2:T(1,128)S(1)}, s32[1,8,6]{1,0,2:T(1,128)}, u32[]{:S(2)}) copy-start(s32[1,8,6]{1,0,2:T(1,128)} %param.6) | copy-start | bytes 580
  130.1 1.1 copy-start.1
  131.3 1.9 %copy-start.2 = (bf16[16,768,128]{2,1,0:T(8,128)(2,1)S(1)}, bf16[16,768,128]{2,1,0:T(8,128)(2,1)}, u32[]{:S(2)}) copy-start(bf16[16,768,128]{2,1,0:T(8,128)(2,1)} %all-gather.3.cloned.1.call-done.all_ref) | copy-start | bytes 9437188
Sparse Core Ops, SparseCore 0:
  87.2 42.8 all-gather.2

commit v2 on v1

v2 whole, which is shorter than its diff:
```python
import functools

import jax
import jax.numpy as jnp
from jax import lax
from jax.experimental import pallas as pl
from jax.experimental.pallas import tpu as pltpu
from jax.sharding import PartitionSpec as P

BLK = 128
SLOT = 8
MESH = pl.DeviceIdType.MESH


def pair_kernel(sizes, wanted_ref, index_ref, all_ref, out_ref, turned, staged):
    pairs, nosv, fblk, npart = sizes
    orbs = 2 * pairs
    half = nosv // 2
    lanes = 2 * nosv
    group = lax.axis_index("orb")
    row = lax.broadcasted_iota(jnp.int32, (lanes, lanes), 0)
    col = lax.broadcasted_iota(jnp.int32, (lanes, lanes), 1)
    inner = row % nosv
    source = (row // nosv) * nosv + (inner % half) * 2 + inner // half
    order = jnp.where(col == source, 1.0, 0.0).astype(jnp.bfloat16)
    for q in range(pairs):
        flipped = lax.dot_general(
            order, all_ref[group * pairs + q], (((1,), (1,)), ((), ())), preferred_element_type=jnp.float32
        ).astype(jnp.bfloat16)
        for s in range(2):
            for b in range(fblk):
                turned[2 * q + s, b] = flipped[s * nosv:(s + 1) * nosv, b * BLK:(b + 1) * BLK]
            turned[2 * q + s, fblk] = jnp.zeros((nosv, BLK), jnp.bfloat16)

    lane = lax.broadcasted_iota(jnp.int32, (half, lanes), 1)
    low = lane < nosv

    @pl.loop(0, npart)
    def _(n):
        w = wanted_ref[group, n]
        slab = w // 2
        odd = (w % 2) == 1
        rhs = all_ref[slab]
        lhs = jnp.concatenate(
            [
                jnp.concatenate(
                    [turned[r, index_ref[w, r * SLOT + e]] for e in range(fblk)], axis=1
                )
                for r in range(orbs)
            ],
            axis=0,
        )
        vals = jnp.dot(lhs, rhs, preferred_element_type=jnp.float32)
        keep_low = jnp.logical_xor(low, odd)
        for r in range(orbs):
            even_rows = vals[r * nosv:r * nosv + half]
            odd_rows = vals[r * nosv + half:(r + 1) * nosv]
            moved = pltpu.roll(jnp.where(odd, even_rows, odd_rows), nosv, 1)
            kept = jnp.where(odd, odd_rows, even_rows)
            staged[r, pl.ds(n, half, stride=npart), :] = jnp.where(keep_low, kept, moved)

    for r in range(orbs):
        for j in range(half):
            out_ref[r, :, j * lanes:(j + 1) * lanes] = staged[
                r, j * npart:(j + 1) * npart, :
            ].astype(jnp.bfloat16)


def pair_integrals(gathered, index, lists, orbs, fblk):
    depth, lanes = gathered.shape[1:]
    pairs, nosv, npart = orbs // 2, lanes // 2, lists.shape[1]
    return pl.pallas_call(
        functools.partial(pair_kernel, (pairs, nosv, fblk, npart)),
        out_shape=jax.ShapeDtypeStruct((orbs, npart, nosv * nosv), jnp.bfloat16),
        in_specs=[
            pl.BlockSpec(memory_space=pltpu.SMEM),
            pl.BlockSpec(memory_space=pltpu.SMEM),
            pl.BlockSpec(memory_space=pltpu.VMEM),
        ],
        out_specs=pl.BlockSpec(memory_space=pltpu.VMEM),
        scratch_shapes=[
            pltpu.VMEM((orbs, fblk + 1, nosv, BLK), jnp.bfloat16),
            pltpu.VMEM((orbs, (nosv // 2) * npart, lanes), jnp.float32),
        ],
        compiler_params=pltpu.CompilerParams(vmem_limit_bytes=48 << 20),
        cost_estimate=pl.CostEstimate(
            flops=2 * npart * orbs * nosv * lanes * depth,
            bytes_accessed=2 * (gathered.size + orbs * npart * nosv * nosv),
            transcendentals=0,
        ),
    )(lists, index, gathered)


def match_index(theirs, own, fblk):
    index = jnp.full(theirs.shape, fblk, jnp.int32)
    for b in range(fblk):
        index = jnp.where(theirs == own[b:b + 1, :], b, index)
    return index


def move_kernel(
    columns, osv_ref, tile_ref, own_tile_ref, rows_ref, all_ref, index_ref,
    rows_v, osv_all, stage, tiles,
    rows_sem, osv_send, osv_recv, tile_send, tile_recv, piece_send, piece_recv,
    out_send, out_recv, far_send, far_recv, fblk,
):
    fits = columns
    levels = fits // 2
    pairs, aod, lanes = osv_ref.shape
    orbs = 2 * pairs
    depth = rows_v.shape[1]
    half = pairs // 2
    me = lax.axis_index("fit")
    g = lax.axis_index("orb")
    z, core = me // 2, me % 2
    sib = z * 2 + 1 - core
    y, x = g // 2, g % 2
    sides = (y * 2 + 1 - x, (1 - y) * 2 + x)
    far = (1 - y) * 2 + 1 - x

    def rows_copy(c):
        here = pl.ds(c * orbs, orbs)
        return pltpu.make_async_copy(rows_ref.at[here], rows_v.at[here], rows_sem.at[c])

    for c in range(fits):
        rows_copy(c).start()

    barrier = pltpu.get_barrier_semaphore()
    for step in range(1, fits):
        pl.semaphore_signal(barrier, inc=1, device_id={"fit": (me + step) % fits}, device_id_type=MESH)
    for peer in (*sides, far):
        pl.semaphore_signal(barrier, inc=1, device_id={"orb": peer}, device_id_type=MESH)
    pl.semaphore_wait(barrier, fits - 1 + 3)

    def osv_copy(shard, way, target, source=None):
        return pltpu.make_async_remote_copy(
            src_ref=osv_all.at[shard] if source is None else source,
            dst_ref=osv_all.at[shard],
            send_sem=osv_send.at[way, shard],
            recv_sem=osv_recv.at[shard],
            device_id={"fit": target},
            device_id_type=MESH,
        )

    def slab(h, d, first, count):
        return all_ref.at[
            pl.ds(h * pairs + first, count), pl.ds(pl.multiple_of(d * depth, 16), depth), :
        ]

    def piece_copy(c):
        return pltpu.make_async_remote_copy(
            src_ref=stage.at[c],
            dst_ref=slab(g, me, 0, pairs),
            send_sem=piece_send.at[c],
            recv_sem=piece_recv.at[me],
            device_id={"fit": c},
            device_id_type=MESH,
        )

    def piece_arrival(d):
        return pltpu.make_async_remote_copy(
            src_ref=stage.at[d],
            dst_ref=slab(g, d, 0, pairs),
            send_sem=piece_send.at[d],
            recv_sem=piece_recv.at[d],
            device_id={"fit": d},
            device_id_type=MESH,
        )

    def out_copy(d, way, h):
        part = slab(h, d, 0, pairs)
        return pltpu.make_async_remote_copy(
            src_ref=part, dst_ref=part,
            send_sem=out_send.at[way, d], recv_sem=out_recv.at[way, d],
            device_id={"orb": sides[way]}, device_id_type=MESH,
        )

    def far_copy(d, way, h):
        part = slab(h, d, half * (1 - way), half)
        return pltpu.make_async_remote_copy(
            src_ref=part, dst_ref=part,
            send_sem=far_send.at[way, d], recv_sem=far_recv.at[way, d],
            device_id={"orb": sides[way]}, device_id_type=MESH,
        )

    def tile_copy(number, peer, slot):
        return pltpu.make_async_remote_copy(
            src_ref=tile_ref, dst_ref=tiles.at[slot],
            send_sem=tile_send.at[number], recv_sem=tile_recv.at[slot],
            device_id={"orb": peer}, device_id_type=MESH,
        )

    low = lax.broadcasted_iota(jnp.int32, (depth, lanes), 1) < lanes // 2

    def project(c, osv, q):
        lhs = rows_v[pl.ds(c * orbs + 2 * q, 2)].reshape(2 * depth, aod)
        vals = jnp.dot(lhs, osv, preferred_element_type=jnp.float32)
        return jnp.where(low, vals[:depth], vals[depth:]).astype(jnp.bfloat16)

    def project_and_send(c):
        osv_copy(c, 0, sib).wait_recv()
        rows_copy(c).wait()
        for q in range(pairs):
            stage[c, q] = project(c, osv_all[c, q], q)
        piece_copy(c).start()

    def within(level):
        return jnp.logical_and(level >= 0, level < levels)

    def at_distance(j, action):
        if j == 0:
            action(me)
            action(sib)
        else:
            for s in (1, -1):
                @pl.when(within(z + s * j))
                def _():
                    action((z + s * j) * 2 + core)
                    action((z + s * j) * 2 + 1 - core)

    def spread(d):
        out_copy(d, 0, g).start()
        out_copy(d, 1, g).start()

    def take_and_spread(d):
        piece_arrival(d).wait_recv()
        spread(d)

    def relay(d):
        out_copy(d, 0, sides[0]).wait_recv()
        far_copy(d, 1, sides[0]).start()
        out_copy(d, 1, sides[1]).wait_recv()
        far_copy(d, 0, sides[1]).start()

    for way, s in ((0, 1), (1, -1)):
        @pl.when(within(z + s))
        def _():
            osv_copy(me, way, me + 2 * s, osv_ref).start()
    osv_copy(me, 2, sib, osv_ref).start()
    for number, peer in enumerate((*sides, far)):
        tile_copy(number, peer, g).start()

    rows_copy(me).wait()
    for q in range(pairs):
        all_ref[g * pairs + q, pl.ds(pl.multiple_of(me * depth, 16), depth), :] = project(
            me, osv_ref[q], q
        )
    spread(me)
    project_and_send(sib)

    for j in range(1, levels):
        for way, s in ((1, 1), (0, -1)):
            @pl.when(within(z + s * j))
            def _():
                shard = (z + s * j) * 2 + core
                osv_copy(shard, way, sib).wait_recv()

                @pl.when(within(z - s))
                def _():
                    osv_copy(shard, way, me - 2 * s).start()
                osv_copy(shard, 2, sib).start()
                rows_copy(shard).wait()
                for q in range(pairs):
                    stage[shard, q] = project(shard, osv_all[shard, q], q)
                piece_copy(shard).start()
        for s in (1, -1):
            @pl.when(within(z + s * j))
            def _():
                project_and_send((z + s * j) * 2 + 1 - core)
        if j == 1:
            take_and_spread(sib)
            for number, peer in enumerate((*sides, far)):
                tile_copy(number, peer, peer).wait_recv()
            tiles[g] = tile_ref[...]
            for h in range(tiles.shape[0]):
                index_ref[h * orbs:(h + 1) * orbs, :] = match_index(
                    tiles[h], own_tile_ref[...], fblk
                )
        else:
            at_distance(j - 1, take_and_spread)
            at_distance(j - 2, relay)
    at_distance(levels - 1, take_and_spread)
    if levels > 1:
        at_distance(levels - 2, relay)
    at_distance(levels - 1, relay)

    for d in range(fits):
        far_copy(d, 1, far).wait_recv()
        far_copy(d, 0, far).wait_recv()
    for d in range(fits):
        for way in range(2):
            out_copy(d, way, g).wait_send()
            far_copy(d, way, sides[1 - way]).wait_send()

        @pl.when(d != me)
        def _():
            piece_copy(d).wait_send()
    for number, peer in enumerate((*sides, far)):
        tile_copy(number, peer, g).wait_send()
    for way, s in ((0, 1), (1, -1)):
        @pl.when(within(z + s))
        def _():
            osv_copy(me, way, me + 2 * s, osv_ref).wait_send()
    osv_copy(me, 2, sib, osv_ref).wait_send()
    for j in range(1, levels):
        for way, s in ((1, 1), (0, -1)):
            @pl.when(within(z + s * j))
            def _():
                shard = (z + s * j) * 2 + core

                @pl.when(within(z - s))
                def _():
                    osv_copy(shard, way, me - 2 * s).wait_send()
                osv_copy(shard, 2, sib).wait_send()


def move(rows, osv, tile, own_tile, fits, fblk):
    pairs, aod, lanes = osv.shape
    orbs = 2 * pairs
    depth = rows.shape[1]
    groups = 4
    dma = pltpu.SemaphoreType.DMA
    full = pl.BlockSpec(memory_space=pltpu.VMEM)

    def kernel(*refs):
        move_kernel(fits, *refs, fblk)

    return pl.pallas_call(
        kernel,
        out_shape=(
            jax.ShapeDtypeStruct((groups * pairs, fits * depth, lanes), jnp.bfloat16),
            jax.ShapeDtypeStruct((groups * orbs, tile.shape[1]), jnp.int32),
        ),
        in_specs=[full, full, full, pl.BlockSpec(memory_space=pl.ANY)],
        out_specs=(full, full),
        scratch_shapes=[
            pltpu.VMEM(rows.shape, jnp.bfloat16),
            pltpu.VMEM((fits, pairs, aod, lanes), jnp.bfloat16),
            pltpu.VMEM((fits, pairs, depth, lanes), jnp.bfloat16),
            pltpu.VMEM((groups, *tile.shape), jnp.int32),
            dma((fits,)),
            dma((3, fits)), dma((fits,)),
            dma((3,)), dma((groups,)),
            dma((fits,)), dma((fits,)),
            dma((2, fits)), dma((2, fits)),
            dma((2, fits)), dma((2, fits)),
        ],
        compiler_params=pltpu.CompilerParams(
            collective_id=0, has_side_effects=True, vmem_limit_bytes=48 << 20
        ),
        cost_estimate=pl.CostEstimate(
            flops=2 * rows.size * lanes, bytes_accessed=4 * rows.size, transcendentals=0
        ),
    )(osv, tile, own_tile, rows)


def exchange(rows, osv):
    own_ints = lax.all_to_all(rows, "fit", split_axis=0, concat_axis=1, tiled=True)
    projected = jnp.einsum(
        "kfa,kao->kfo", own_ints, osv, preferred_element_type=jnp.float32
    ).astype(jnp.bfloat16)
    return lax.all_gather(side_by_side(projected), "orb", axis=0, tiled=True)


def side_by_side(pieces):
    count, rows, width = pieces.shape
    return (
        pieces.reshape(count // 2, 2, rows, width)
        .transpose(0, 2, 1, 3)
        .reshape(count // 2, rows, 2 * width)
    )


def per_device(sizes, half_ints, osv_coef, fit_blocks, partner_list):
    fits, groups = sizes
    rows, osv, blocks = half_ints[0], osv_coef[0], fit_blocks[0]
    orbs, fblk = blocks.shape
    width = -(-orbs * SLOT // 128) * 128
    padded = jnp.pad(blocks, ((0, 0), (0, SLOT - fblk)), constant_values=-1)
    tile = jnp.tile(padded, (1, width // SLOT))
    own_tile = jnp.pad(
        jnp.repeat(padded.T, SLOT, axis=1), ((0, 0), (0, width - orbs * SLOT)), constant_values=-2
    )
    if groups == 4 and fits % 2 == 0 and rows.shape[1] % 16 == 0:
        gathered, index = move(rows, side_by_side(osv), tile, own_tile, fits, fblk)
    else:
        gathered = exchange(rows, osv)
        index = match_index(lax.all_gather(tile, "orb", axis=0, tiled=True), own_tile, fblk)
    return pair_integrals(gathered, index, partner_list[0], orbs, fblk)[None]


def solution(mesh):
    return jax.shard_map(
        functools.partial(per_device, (mesh.shape["fit"], mesh.shape["orb"])),
        mesh=mesh,
        in_specs=(
            P("orb", None, "fit", None),
            P("orb", "fit", None, None),
            P("orb", "fit", None),
            P("fit", None, None),
        ),
        out_specs=P("orb", "fit", None, None),
        check_vma=False,
    )
```

time: 153 us -> 70.1 us (0.46)
  blocking collectives: 86.1 us -> 0 us
  Pallas kernels: 13 us -> 67.7 us
  waiting for transfers between devices: 33.6 us -> 0 us
  between operations: 13.5 us -> 0.04 us
  local copies, waits for them, and re-layouts: 5.58 us -> 2.23 us
    all_to_all x1 -> x0, blocking collectives: 78 us -> none  [exchange(): lax.all_to_all(rows, 'fit', split_axis=0, concat_axis=1, tiled=True)]
    pallas_call x0 -> x1, Pallas kernels: none -> 54.5 us  [move(): pl.pallas_call(kernel, out_shape=(jax.ShapeDtypeStruct((groups * pairs, f...]
    all_gather x1 -> x0, waiting for transfers between devices: 33.6 us -> none  [exchange(): return (own, lax.all_gather(own, 'orb', axis=0, tiled=True))]
    all_gather x1 -> x0, blocking collectives: 8.15 us -> none  [per_device(): all_blocks = lax.all_gather(own_blocks, 'orb', axis=0, tiled=True)]
    unnamed x9 -> x3, local copies, waits for them, and re-layouts: 3.11 us -> 0.78 us
  transfers between devices with their start and end apart: 1 -> 0, of which waited for: 1 -> 0; matrix products, arithmetic and copies ran while one was open for 1% -> 0% of each run, Pallas kernels for 0% -> 0%
where the time goes in v2:
time: 70.1 us; the launch traced here: 70 us
  Pallas kernels  67.7 us (97%)
  local copies, waits for them, and re-layouts  2.23 us (3%)
    pallas_call x1, Pallas kernels, move(): pl.pallas_call(kernel, out_shape=(jax.ShapeDtypeStruct((groups * pairs, f...  54.5 us
    pallas_call x1, Pallas kernels, pair_integrals(): pl.pallas_call(functools.partial(pair_kernel, (pairs, nosv, fblk, npart))...  13.2 us

profile of v2, /device:TPU:0, one launch (start us, length us, event | category | flops | bytes accessed | tf_op | source)
XLA Modules:
  0.0 70.0 jit_solution(15658960761860299955)
XLA Ops:
  0.0 0.0 copy-start
  0.0 0.8 %copy.8 = s32[1,8,6]{2,1,0:T(8,128)S(1)} copy(s32[1,8,6]{1,0,2:T(1,128)} %param.6) | data formatting | bytes 384 | tf_op args[2]
  0.8 0.1 copy.9
  0.9 0.1 broadcast_in_dim.6
  0.9 0.1 reshape.11
  1.0 0.1 tile.10.refs_1_
  1.1 1.1 %copy.10.refs_0_ = bf16[4,256,128]{2,1,0:T(8,128)(2,1)S(1)} copy(bf16[4,256,128]{1,2,0:T(8,128)(2,1)} %bitcast.13) | data formatting | bytes 524288 | tf_op jit(solution)/shard_map/reshape | solution.py:370
  2.3 54.5 %shard_map.46 = (bf16[16,768,128]{2,1,0:T(8,128)(2,1)S(1)}, s32[32,128]{1,0:T(8,128)S(1)}) custom-call(bf16[4,256,128]{2,1,0:T(8,128)(2,1)S(1)} %copy.10.refs_0_, s32[8,128]{1,0:T(8,128)S(1)} %tile.10.refs_1_, s32[8,128]{1,0:T(8,128)S(1)} %pad.9.refs_2_, bf16[64,96,256]{2,1,0:T(8,128)(2,1)} %bitcast.12), custom_call_target="tpu_custom_call" | custom-call | flops 402653184 | bytes 6291456 | tf_op jit(solution)/shard_map/pallas_call | solution.py:328
  56.8 0.0 copy-done
  56.8 13.2 %shard_map.47 = bf16[8,24,4096]{2,1,0:T(8,128)(2,1)} custom-call(s32[4,24]{1,0:T(4,128)S(1)} %bitcast.11, s32[32,128]{1,0:T(8,128)S(1)} %get-tuple-element.7.index_ref, bf16[16,768,128]{2,1,0:T(8,128)(2,1)S(1)} %get-tuple-element.8.all_ref), custom_call_target="tpu_custom_call" | custom-call | flops 2415919104 | bytes 4718592 | tf_op jit(solution)/shard_map/pallas_call | solution.py:72
  (3 shorter events, 0.0 us)
Async XLA Ops:
  0.0 56.8 %copy-start = (s32[1,4,24]{2,1,0:T(4,128)S(1)}, s32[1,4,24]{2,1,0:T(4,128)}, u32[]{:S(2)}) copy-start(s32[1,4,24]{2,1,0:T(4,128)} %param.7) | copy-start | bytes 1156

commit v3 on v2

--- a/solution.py
+++ b/solution.py
@@ -35,7 +35,7 @@
     lane = lax.broadcasted_iota(jnp.int32, (half, lanes), 1)
     low = lane < nosv
 
-    @pl.loop(0, npart)
+    @pl.loop(0, npart, unroll=12)
     def _(n):
         w = wanted_ref[group, n]
         slab = w // 2
@@ -132,12 +132,35 @@
         pl.semaphore_signal(barrier, inc=1, device_id={"orb": peer}, device_id_type=MESH)
     pl.semaphore_wait(barrier, fits - 1 + 3)
 
+    parts = 2
+    size = pairs // parts
+
+    class Parts:
+        def __init__(self, *copies):
+            self.copies = copies
+
+        def start(self):
+            for copy in self.copies:
+                copy.start()
+
+        def wait_recv(self):
+            for copy in self.copies:
+                copy.wait_recv()
+
+        def wait_send(self):
+            for copy in self.copies:
+                copy.wait_send()
+
     def osv_copy(shard, way, target, source=None):
-        return pltpu.make_async_remote_copy(
-            src_ref=osv_all.at[shard] if source is None else source,
-            dst_ref=osv_all.at[shard],
-            send_sem=osv_send.at[way, shard],
-            recv_sem=osv_recv.at[shard],
+        return Parts(*(osv_part(shard, way, target, source, p) for p in range(parts)))
+
+    def osv_part(shard, way, target, source, p):
+        some = pl.ds(p * size, size)
+        return pltpu.make_async_remote_copy(
+            src_ref=osv_all.at[shard, some] if source is None else source.at[some],
+            dst_ref=osv_all.at[shard, some],
+            send_sem=osv_send.at[way, shard, p],
+            recv_sem=osv_recv.at[shard, p],
             device_id={"fit": target},
             device_id_type=MESH,
         )
@@ -172,7 +195,7 @@
         return pltpu.make_async_remote_copy(
             src_ref=part, dst_ref=part,
             send_sem=out_send.at[way, d], recv_sem=out_recv.at[way, d],
-            device_id={"orb": sides[way]}, device_id_type=MESH,
+            device_id={"orb": (*sides, far)[way]}, device_id_type=MESH,
         )
 
     def far_copy(d, way, h):
@@ -209,28 +232,49 @@
 
     def at_distance(j, action):
         if j == 0:
-            action(me)
-            action(sib)
+            action(me, 0)
+            action(sib, 0)
         else:
             for s in (1, -1):
                 @pl.when(within(z + s * j))
                 def _():
-                    action((z + s * j) * 2 + core)
-                    action((z + s * j) * 2 + 1 - core)
-
-    def spread(d):
+                    action((z + s * j) * 2 + core, j)
+                    action((z + s * j) * 2 + 1 - core, j)
+
+    cutoff = 0
+
+    def spread(d, j):
+        if j >= cutoff:
+            out_copy(d, 2, g).start()
         out_copy(d, 0, g).start()
         out_copy(d, 1, g).start()
 
-    def take_and_spread(d):
+    def take_and_spread(d, j):
         piece_arrival(d).wait_recv()
-        spread(d)
-
-    def relay(d):
-        out_copy(d, 0, sides[0]).wait_recv()
-        far_copy(d, 1, sides[0]).start()
-        out_copy(d, 1, sides[1]).wait_recv()
-        far_copy(d, 0, sides[1]).start()
+        spread(d, j)
+
+    def relay(d, j):
+        if j < cutoff:
+            out_copy(d, 0, sides[0]).wait_recv()
+            far_copy(d, 1, sides[0]).start()
+            out_copy(d, 1, sides[1]).wait_recv()
+            far_copy(d, 0, sides[1]).start()
+
+    def last_arrivals(d, j):
+        if j < cutoff:
+            far_copy(d, 1, far).wait_recv()
+            far_copy(d, 0, far).wait_recv()
+        else:
+            for way, h in enumerate((*sides, far)):
+                out_copy(d, way, h).wait_recv()
+
+    def last_sends(d, j):
+        for way in range(2):
+            out_copy(d, way, g).wait_send()
+            if j < cutoff:
+                far_copy(d, way, sides[1 - way]).wait_send()
+        if j >= cutoff:
+            out_copy(d, 2, g).wait_send()
 
     for way, s in ((0, 1), (1, -1)):
         @pl.when(within(z + s))
@@ -245,20 +289,14 @@
         all_ref[g * pairs + q, pl.ds(pl.multiple_of(me * depth, 16), depth), :] = project(
             me, osv_ref[q], q
         )
-    spread(me)
+    spread(me, 0)
     project_and_send(sib)
 
-    for j in range(1, levels):
-        for way, s in ((1, 1), (0, -1)):
+    def project_at(j):
+        for s in (1, -1):
             @pl.when(within(z + s * j))
             def _():
                 shard = (z + s * j) * 2 + core
-                osv_copy(shard, way, sib).wait_recv()
-
-                @pl.when(within(z - s))
-                def _():
-                    osv_copy(shard, way, me - 2 * s).start()
-                osv_copy(shard, 2, sib).start()
                 rows_copy(shard).wait()
                 for q in range(pairs):
                     stage[shard, q] = project(shard, osv_all[shard, q], q)
@@ -267,8 +305,23 @@
             @pl.when(within(z + s * j))
             def _():
                 project_and_send((z + s * j) * 2 + 1 - core)
+
+    for j in range(1, levels):
+        for p in range(parts):
+            for way, s in ((1, 1), (0, -1)):
+                @pl.when(within(z + s * j))
+                def _():
+                    shard = (z + s * j) * 2 + core
+                    osv_part(shard, way, sib, None, p).wait_recv()
+
+                    @pl.when(within(z - s))
+                    def _():
+                        osv_part(shard, way, me - 2 * s, None, p).start()
+                    osv_part(shard, 2, sib, None, p).start()
         if j == 1:
-            take_and_spread(sib)
+            project_at(j)
+            piece_arrival(sib).wait_recv()
+            spread(sib, 0)
             for number, peer in enumerate((*sides, far)):
                 tile_copy(number, peer, peer).wait_recv()
             tiles[g] = tile_ref[...]
@@ -276,22 +329,27 @@
                 index_ref[h * orbs:(h + 1) * orbs, :] = match_index(
                     tiles[h], own_tile_ref[...], fblk
                 )
+            relay(me, 0)
+        elif j == 2:
+            at_distance(j - 1, take_and_spread)
+            relay(sib, 0)
+            project_at(j)
         else:
+            project_at(j)
             at_distance(j - 1, take_and_spread)
             at_distance(j - 2, relay)
     at_distance(levels - 1, take_and_spread)
-    if levels > 1:
+    if levels > 2:
         at_distance(levels - 2, relay)
+    if levels == 2:
+        relay(sib, 0)
     at_distance(levels - 1, relay)
 
+    for j in range(levels):
+        at_distance(j, last_arrivals)
+    for j in range(levels):
+        at_distance(j, last_sends)
     for d in range(fits):
-        far_copy(d, 1, far).wait_recv()
-        far_copy(d, 0, far).wait_recv()
-    for d in range(fits):
-        for way in range(2):
-            out_copy(d, way, g).wait_send()
-            far_copy(d, way, sides[1 - way]).wait_send()
-
         @pl.when(d != me)
         def _():
             piece_copy(d).wait_send()
@@ -339,10 +397,10 @@
             pltpu.VMEM((fits, pairs, depth, lanes), jnp.bfloat16),
             pltpu.VMEM((groups, *tile.shape), jnp.int32),
             dma((fits,)),
-            dma((3, fits)), dma((fits,)),
+            dma((3, fits, 2)), dma((fits, 2)),
             dma((3,)), dma((groups,)),
             dma((fits,)), dma((fits,)),
-            dma((2, fits)), dma((2, fits)),
+            dma((3, fits)), dma((3, fits)),
             dma((2, fits)), dma((2, fits)),
         ],
         compiler_params=pltpu.CompilerParams(

time: 70.1 us -> 64.5 us (0.920)
  Pallas kernels: 67.7 us -> 62 us
    pallas_call x1, Pallas kernels: 13.2 us -> 7.95 us  [pair_integrals(): pl.pallas_call(functools.partial(pair_kernel, (pairs, nosv, fblk, npart))...]
where the time goes in v3:
time: 64.5 us; the launch traced here: 64.3 us
  Pallas kernels  62 us (96%)
  local copies, waits for them, and re-layouts  2.23 us (3%)
    pallas_call x1, Pallas kernels, move(): pl.pallas_call(kernel, out_shape=(jax.ShapeDtypeStruct((groups * pairs, f...  54.1 us
    pallas_call x1, Pallas kernels, pair_integrals(): pl.pallas_call(functools.partial(pair_kernel, (pairs, nosv, fblk, npart))...  7.95 us

profile of v3, /device:TPU:0, one launch (start us, length us, event | category | flops | bytes accessed | tf_op | source)
XLA Modules:
  0.0 64.3 jit_solution(8023032162144967949)
XLA Ops:
  0.0 0.0 copy-start
  0.0 0.8 %copy.8 = s32[1,8,6]{2,1,0:T(8,128)S(1)} copy(s32[1,8,6]{1,0,2:T(1,128)} %param.6) | data formatting | bytes 384 | tf_op args[2]
  0.8 0.1 copy.9
  0.9 0.1 broadcast_in_dim.6
  0.9 0.1 reshape.11
  1.0 0.1 tile.10.refs_1_
  1.1 1.1 %copy.10.refs_0_ = bf16[4,256,128]{2,1,0:T(8,128)(2,1)S(1)} copy(bf16[4,256,128]{1,2,0:T(8,128)(2,1)} %bitcast.13) | data formatting | bytes 524288 | tf_op jit(solution)/shard_map/reshape | solution.py:428
  2.3 54.1 %shard_map.46 = (bf16[16,768,128]{2,1,0:T(8,128)(2,1)S(1)}, s32[32,128]{1,0:T(8,128)S(1)}) custom-call(bf16[4,256,128]{2,1,0:T(8,128)(2,1)S(1)} %copy.10.refs_0_, s32[8,128]{1,0:T(8,128)S(1)} %tile.10.refs_1_, s32[8,128]{1,0:T(8,128)S(1)} %pad.9.refs_2_, bf16[64,96,256]{2,1,0:T(8,128)(2,1)} %bitcast.12), custom_call_target="tpu_custom_call" | custom-call | flops 402653184 | bytes 6291456 | tf_op jit(solution)/shard_map/pallas_call | solution.py:386
  56.3 0.0 copy-done
  56.3 8.0 %shard_map.47 = bf16[8,24,4096]{2,1,0:T(8,128)(2,1)} custom-call(s32[4,24]{1,0:T(4,128)S(1)} %bitcast.11, s32[32,128]{1,0:T(8,128)S(1)} %get-tuple-element.7.index_ref, bf16[16,768,128]{2,1,0:T(8,128)(2,1)S(1)} %get-tuple-element.8.all_ref), custom_call_target="tpu_custom_call" | custom-call | flops 2415919104 | bytes 4718592 | tf_op jit(solution)/shard_map/pallas_call | solution.py:72
  (3 shorter events, 0.0 us)
Async XLA Ops:
  0.0 56.3 %copy-start = (s32[1,4,24]{2,1,0:T(4,128)S(1)}, s32[1,4,24]{2,1,0:T(4,128)}, u32[]{:S(2)}) copy-start(s32[1,4,24]{2,1,0:T(4,128)} %param.7) | copy-start | bytes 1156
